TPU v7x, 256 devices: a whole 4x4x8 slice. The times are simulated.
256 devices in a mesh: prompt: 16 (over x, y), comp: 16 (over z, core).
Axes of the slice: x: 4, y: 4, z: 8, core: 2. Of those that a mesh axis runs over, the one named last changes fastest.
Arguments:
- q_raw: bfloat16 [16, 2048, 8192], P('prompt', 'comp'), may hold values from -8 to 8
- d_out: bfloat16 [16, 2048, 8192], P('prompt', 'comp'), may hold values from -6 to 6
- k_prompt: bfloat16 [16, 1024, 1024], P('prompt', 'comp'), may hold values from -8 to 8
- v_prompt: bfloat16 [16, 1024, 1024], P('prompt', 'comp'), may hold values from -6 to 6
- k_comp: bfloat16 [16, 2048, 1024], P('prompt', 'comp'), may hold values from -6 to 6
- v_comp: bfloat16 [16, 2048, 1024], P('prompt', 'comp'), may hold values from -6 to 6
- lengths: int32 [16, 16, 4], P('prompt', 'comp'), may hold values from 1 to 64, 128 in all within a row
- q_gain: float32 [128], replicated, may hold values from 0.5 to 4.5
- k_gain: float32 [128], replicated, may hold values from 0.5 to 4.5
Outputs:
- d_q_raw: bfloat16 [16, 2048, 8192], P('prompt', 'comp')
- d_k_comp: bfloat16 [16, 2048, 1024], P('prompt', 'comp')
- d_v_comp: bfloat16 [16, 2048, 1024], P('prompt', 'comp')
- d_k_prompt: bfloat16 [16, 1024, 1024], P('prompt', 'comp')
- d_v_prompt: bfloat16 [16, 1024, 1024], P('prompt', 'comp')
- d_q_gain: float32 [128], replicated
- d_k_gain: float32 [128], replicated
Inputs may be any that keep to these rules, and one draw needn't show every extreme that they name: Each row of lengths sums to 128, and its largest entry is 64.
All inputs are finite; a program needn't handle non-finite values.
Results may differ from a plain program's by a relative error of at most 0.027.
The roundings to bfloat16 on the way count: a program that leaves them out, or rounds other values in their place, can miss the bound.
Values may be sent and summed in bfloat16 or wider, within the bound.
A program may use at most 128 MiB of HBM per device.

v0:
```python
import math

import jax
import jax.numpy as jnp
from jax import lax
from jax.sharding import PartitionSpec as P

H = 64
KVH = 8
HD = 128


epsilon = 1e-06


def norm_rows(values, gain):
    values = values.astype(jnp.float32)
    inverse = lax.rsqrt(jnp.mean(values * values, axis=-1, keepdims=True) + epsilon)
    return (values * inverse * gain, inverse)


def norm_back(values, inverse, gain, grad):
    values = values.astype(jnp.float32)
    scaled = grad * gain
    inner = jnp.mean(values * scaled, axis=-1, keepdims=True)
    dx = inverse * scaled - values * inverse * inverse * inverse * inner
    dgain = jnp.sum((grad * values * inverse).reshape(-1, values.shape[-1]), axis=0)
    return (dx, dgain)


def segment_ids(lengths, slots):
    ends = jnp.cumsum(lengths)
    places = jnp.arange(slots, dtype=jnp.int32)
    return jnp.sum((places[:, None] >= ends[None, :]).astype(jnp.int32), axis=1)


def body(q_raw, d_out, k_prompt, v_prompt, k_comp, v_comp, lengths, q_gain, k_gain):
    f32 = jnp.float32
    bf16 = jnp.bfloat16
    slots = q_raw.shape[1]
    page = k_prompt.shape[1]
    group = H // KVH
    scale = 1.0 / math.sqrt(HD)
    prompt_k, prompt_v = (
        lax.all_gather(k_prompt[0], "comp", axis=0, tiled=True),
        lax.all_gather(v_prompt[0], "comp", axis=0, tiled=True),
    )
    span = prompt_k.shape[0]
    query_raw = q_raw[0].reshape(slots, KVH, group, HD)
    query_norm, query_inv = norm_rows(query_raw, q_gain)
    query = query_norm.astype(bf16)
    prefix_keys = norm_rows(prompt_k.reshape(span, KVH, HD), k_gain)[0].astype(bf16)
    prefix_vals = prompt_v.reshape(span, KVH, HD)
    own_raw = k_comp[0].reshape(slots, KVH, HD)
    own_norm, own_inv = norm_rows(own_raw, k_gain)
    own_keys = own_norm.astype(bf16)
    own_vals = v_comp[0].reshape(slots, KVH, HD)
    grad_out = d_out[0].reshape(slots, KVH, group, HD)
    seg = segment_ids(lengths[0, 0], slots)
    places = jnp.arange(slots, dtype=jnp.int32)
    visible = (seg[:, None] == seg[None, :]) & (places[None, :] <= places[:, None])
    query_heads = jnp.moveaxis(query, 1, 0)
    grad_heads = jnp.moveaxis(grad_out, 1, 0)
    prefix_key_heads = jnp.moveaxis(prefix_keys, 1, 0)
    prefix_val_heads = jnp.moveaxis(prefix_vals, 1, 0)
    own_key_heads = jnp.moveaxis(own_keys, 1, 0)
    own_val_heads = jnp.moveaxis(own_vals, 1, 0)

    def head_pass(items):
        q_head, g_head, pk_head, pv_head, ok_head, ov_head = items
        score_p = jnp.einsum("sgd,td->gst", q_head, pk_head, preferred_element_type=f32) * scale
        score_c = jnp.einsum("sgd,td->gst", q_head, ok_head, preferred_element_type=f32) * scale
        top = jnp.maximum(
            jnp.max(score_p, axis=-1), jnp.max(jnp.where(visible, score_c, -1e30), axis=-1)
        )
        total = jnp.sum(jnp.exp(score_p - top[..., None]), axis=-1)
        total = total + jnp.sum(jnp.where(visible, jnp.exp(score_c - top[..., None]), 0.0), axis=-1)
        lse = top + jnp.log(total)
        prob_p = jnp.exp(score_p - lse[..., None])
        prob_c = jnp.where(visible, jnp.exp(score_c - lse[..., None]), 0.0)
        probb_p = prob_p.astype(bf16)
        probb_c = prob_c.astype(bf16)
        output = jnp.einsum("gst,td->sgd", probb_p, pv_head, preferred_element_type=f32)
        output = output + jnp.einsum("gst,td->sgd", probb_c, ov_head, preferred_element_type=f32)
        delta = jnp.transpose(jnp.sum(g_head * output, axis=-1), (1, 0))
        dprob_p = jnp.einsum("sgd,td->gst", g_head, pv_head, preferred_element_type=f32)
        dprob_c = jnp.einsum("sgd,td->gst", g_head, ov_head, preferred_element_type=f32)
        dsb_p = (prob_p * (dprob_p - delta[..., None])).astype(bf16)
        dsb_c = (prob_c * (dprob_c - delta[..., None])).astype(bf16)
        d_query = jnp.einsum("gst,td->sgd", dsb_p, pk_head, preferred_element_type=f32)
        d_query = (
            d_query + jnp.einsum("gst,td->sgd", dsb_c, ok_head, preferred_element_type=f32)
        ) * scale
        dk_own = jnp.einsum("gst,sgd->td", dsb_c, q_head, preferred_element_type=f32) * scale
        dv_own = jnp.einsum("gst,sgd->td", probb_c, g_head, preferred_element_type=f32)
        dk_prefix = jnp.einsum("gst,sgd->td", dsb_p, q_head, preferred_element_type=f32) * scale
        dv_prefix = jnp.einsum("gst,sgd->td", probb_p, g_head, preferred_element_type=f32)
        extra = (dk_prefix, dv_prefix)
        return (d_query, dk_own, dv_own, lse, delta) + extra

    res = lax.map(
        head_pass,
        (query_heads, grad_heads, prefix_key_heads, prefix_val_heads, own_key_heads, own_val_heads),
    )
    d_query = jnp.moveaxis(res[0], 0, 1)
    dk_own = jnp.moveaxis(res[1], 0, 1)
    dv_own = jnp.moveaxis(res[2], 0, 1)
    dk_prefix = jnp.moveaxis(res[5], 0, 1)
    dv_prefix = jnp.moveaxis(res[6], 0, 1)
    terms = jnp.concatenate(
        [dk_prefix.reshape(span, KVH * HD), dv_prefix.reshape(span, KVH * HD)], axis=1
    )
    summed = lax.psum_scatter(
        terms.astype(jnp.bfloat16), "comp", scatter_dimension=0, tiled=True
    ).astype(jnp.float32)
    dk_sum = summed[:, : KVH * HD].reshape(page, KVH, HD)
    dv_sum = summed[:, KVH * HD :]
    local_raw = k_prompt[0].reshape(page, KVH, HD)
    local_inv = norm_rows(local_raw, k_gain)[1]
    dk_local, gain_kp = norm_back(local_raw, local_inv, k_gain, dk_sum)
    dq_raw, gain_q = norm_back(query_raw, query_inv, q_gain, d_query)
    dk_raw, gain_k = norm_back(own_raw, own_inv, k_gain, dk_own)
    gain_q_all, gain_k_all = lax.psum((gain_q, gain_k + gain_kp), ("prompt", "comp"))
    return (
        dq_raw.reshape(1, slots, H * HD).astype(bf16),
        dk_raw.reshape(1, slots, KVH * HD).astype(bf16),
        dv_own.reshape(1, slots, KVH * HD).astype(bf16),
        dk_local.reshape(1, page, KVH * HD).astype(bf16),
        dv_sum.reshape(1, page, KVH * HD).astype(bf16),
        gain_q_all,
        gain_k_all,
    )


def solution(mesh):
    in_specs = (
        P("prompt", "comp", None),
        P("prompt", "comp", None),
        P("prompt", "comp", None),
        P("prompt", "comp", None),
        P("prompt", "comp", None),
        P("prompt", "comp", None),
        P("prompt", "comp", None),
        P(),
        P(),
    )
    out_specs = (
        P("prompt", "comp", None),
        P("prompt", "comp", None),
        P("prompt", "comp", None),
        P("prompt", "comp", None),
        P("prompt", "comp", None),
        P(),
        P(),
    )
    return jax.shard_map(body, mesh=mesh, in_specs=in_specs, out_specs=out_specs, check_vma=False)
```

profile of v0, /device:TPU:1, one launch (start us, length us, event | category | flops | bytes accessed | tf_op | source)
XLA Modules:
  0.0 423.5 jit_solution(16189464182558958890)
XLA Ops:
  9.9 1.8 copy.103
  11.7 3.2 copy.102
  14.9 4.3 %copy.98 = f32[1,128,8192]{1,2,0:T(8,128)} copy(bf16[1,128,8192]{2,1,0:T(8,128)(2,1)} %param.11) | data formatting | bytes 6291456 | tf_op jit(solution)/shard_map/convert_element_type | solution.py:17
  19.6 2.9 multiply_reduce_fusion.1
  23.3 2.1 fusion.81
  25.5 28.3 %all-gather.5.cloned.1.call-done = bf16[1,1024,1024]{2,1,0:T(8,128)(2,1)} async-done(((bf16[1,64,1024]{2,1,0:T(8,128)(2,1)}), bf16[1,1024,1024]{2,1,0:T(8,128)(2,1)}) %all-gather.5.cloned.1.call-update) | async-done | bytes 2097168 | tf_op jit(solution)/shard_map/all_gather | solution.py:45
  53.8 4.0 copy.99
  57.8 2.1 fusion.76
  59.9 3.7 fusion.82
  63.6 30.1 %all-gather.7.cloned.1.call-done = bf16[1,1024,1024]{2,1,0:T(8,128)(2,1)} async-done(((bf16[1,64,1024]{2,1,0:T(8,128)(2,1)}), bf16[1,1024,1024]{2,1,0:T(8,128)(2,1)}) %all-gather.7.cloned.1.call-update) | async-done | bytes 2097168 | tf_op jit(solution)/shard_map/all_gather | solution.py:46
  93.7 4.0 copy.101
  97.7 173.0 %while.19 = (s32[]{:T(128)}, f32[8,128,8,128]{1,3,2,0:T(8,128)}, f32[8,128,128]{1,2,0:T(8,128)S(1)}, bf16[8,128,128]{2,1,0:T(8,128)(2,1)}, bf16[8,1024,128]{2,1,...) while((s32[]{:T(128)}, f32[8,128,8,128]{1,3,2,0:T(8,128)}, ...), condition=%wide.region_11.12_spmd.clone, body=%wide.region_5.11_spmd.clone.sunk | while | flops 1831925760 | bytes 73073368 | solution.py:101
  103.0 2.1 fusion.160
  108.6 3.5 fusion.162
  115.1 2.4 fusion.168
  124.6 2.1 fusion.160
  130.3 3.5 fusion.162
  136.8 2.4 fusion.168
  139.1 1.8 fusion.165
  146.2 2.1 fusion.160
  151.9 3.5 fusion.162
  158.4 2.4 fusion.168
  160.8 1.8 fusion.165
  167.9 2.1 fusion.160
  173.5 3.5 fusion.162
  180.0 2.4 fusion.168
  182.4 1.8 fusion.165
  189.5 2.1 fusion.160
  195.2 3.5 fusion.162
  201.7 2.4 fusion.168
  204.1 1.8 fusion.165
  211.2 2.1 fusion.160
  216.8 3.5 fusion.162
  223.3 2.4 fusion.168
  225.7 1.8 fusion.165
  232.8 2.1 fusion.160
  238.4 3.5 fusion.162
  244.9 2.4 fusion.168
  254.4 2.1 fusion.160
  260.0 3.5 fusion.162
  266.5 2.4 fusion.168
  268.9 1.8 fusion.165
  270.7 2.8 copy_bitcast_fusion
  273.5 2.4 pad_maximum_fusion
  279.9 5.9 %fusion.80 = (f32[128]{0:T(128)S(1)}, f32[128,8,8]{0,2,1:T(8,128)S(1)}) fusion(f32[128,8,8,128]{0,3,2,1:T(8,128)} %bitcast.319, f32[8,128,8,128]{1,3,2,0:T(8,128)} %get-tuple-element.78, f32[128,8,8]{0,2,1:T(8,128)S(1)} %add_rsqrt_fusion.2, f32[128]{0:T(128)S(1)} %copy-done.10), kind=kLoop, calls=%fused_computation.99 | loop fusion | flops 6283136 | bytes 8455168 | tf_op jit(solution)/shard_map/reduce_sum | solution.py:27
  287.5 2.9 copy.125
  290.4 43.3 %reduce-scatter.2.cloned.1.call-done = bf16[64,2048]{1,0:T(8,128)(2,1)} async-done(((bf16[1024,2048]{1,0:T(8,128)(2,1)}), bf16[64,2048]{1,0:T(8,128)(2,1)}) %reduce-scatter.2.cloned.1.call-update) | async-done | bytes 262160 | tf_op jit(solution)/shard_map/reduce_scatter | solution.py:113
  336.0 79.9 %all-reduce = (f32[128]{0:T(128)}, f32[128]{0:T(128)}) all-reduce(f32[128]{0:T(128)S(1)} %get-tuple-element.185, f32[128]{0:T(128)S(1)} %add.90), channel_id=1, replica_groups=mesh['prompt'=16,'comp'=16] {'prompt','comp'}, use_global_device_ids=true, to_apply=%region_18.19 | all-reduce | flops 256 | bytes 2048 | tf_op jit(solution)/shard_map/psum | solution.py:123
  (234 shorter events, 110.0 us)
Async XLA Ops:
  7.2 46.6 %all-gather.5.cloned.1.call-start = ((), (), s32[]{:S(2)}) async-start(), calls=%async_computation.2 | async-start | bytes 2228224 | tf_op jit(solution)/shard_map/all_gather | solution.py:45
  7.9 85.8 %all-gather.7.cloned.1.call-start = ((), (), s32[]{:S(2)}) async-start(), calls=%async_computation.3 | async-start | bytes 2228224 | tf_op jit(solution)/shard_map/all_gather | solution.py:46
  8.7 325.0 %reduce-scatter.2.cloned.1.call-start = ((), (), s32[]{:S(2)}) async-start(), calls=%async_computation.1 | async-start | bytes 4456448 | tf_op jit(solution)/shard_map/reduce_scatter | solution.py:113
  14.9 4.3 %copy-start.11 = (s32[1,1,4]{2,1,0:T(1,128)S(1)}, s32[1,1,4]{2,1,0:T(1,128)}, u32[]{:S(2)}) copy-start(s32[1,1,4]{2,1,0:T(1,128)} %param.17) | copy-start | bytes 52
  14.9 7.6 %copy-start.9 = (f32[128]{0:T(128)S(1)}, f32[128]{0:T(128)}, u32[]{:S(2)}) copy-start(f32[128]{0:T(128)} %param.19) | copy-start | bytes 1540
  14.9 8.4 %copy-start.10 = (f32[128]{0:T(128)S(1)}, f32[128]{0:T(128)}, u32[]{:S(2)}) copy-start(f32[128]{0:T(128)} %param.18) | copy-start | bytes 1540
  19.4 4.0 copy-start.2
  101.0 4.1 copy-start
  108.6 3.6 copy-start.1
  122.6 4.1 copy-start
  130.2 3.6 copy-start.1
  144.3 4.1 copy-start
  151.9 3.6 copy-start.1
  165.9 4.1 copy-start
  173.5 3.6 copy-start.1
  187.5 4.1 copy-start
  195.2 3.6 copy-start.1
  209.2 4.1 copy-start
  216.8 3.6 copy-start.1
  230.8 4.1 copy-start
  238.4 3.6 copy-start.1
  252.4 4.1 copy-start
  260.0 3.6 copy-start.1
  275.9 0.9 copy-start.5
  276.0 1.8 copy-start.8
  279.9 5.9 %copy-start.3 = (f32[1,128,8192]{1,2,0:T(8,128)S(1)}, f32[1,128,8192]{1,2,0:T(8,128)}, u32[]{:S(2)}) copy-start(f32[1,128,8192]{1,2,0:T(8,128)} %copy.98) | copy-start | bytes 12582916
  279.9 6.0 %copy-start.4 = (f32[8,128,8,128]{1,3,2,0:T(8,128)S(1)}, f32[8,128,8,128]{1,3,2,0:T(8,128)}, u32[]{:S(2)}) copy-start(f32[8,128,8,128]{1,3,2,0:T(8,128)} %get-tuple-element.78) | copy-start | bytes 12582916
  287.4 48.1 %copy-start.6 = (f32[8,8,8,128]{3,2,1,0:T(8,128)S(1)}, f32[8,8,8,128]{3,2,1,0:T(8,128)}, u32[]{:S(2)}) copy-start(f32[8,8,8,128]{3,2,1,0:T(8,128)} %copy.149) | copy-start | bytes 786436
  333.6 82.5 %copy-start.7 = (bf16[64,2048]{1,0:T(8,128)(2,1)S(1)}, bf16[64,2048]{1,0:T(8,128)(2,1)}, u32[]{:S(2)}) copy-start(bf16[64,2048]{1,0:T(8,128)(2,1)} %reduce-scatter.2.cloned.1.call-done) | copy-start | bytes 786436
Sparse Core Ops, SparseCore 0:
  9.8 43.9 all-gather.4
  55.6 38.0 all-gather.6
  276.1 57.4 reduce-scatter.1
where the time goes:
time: 427 us; the launch traced here: 424 us
  matrix products  162 us (38%)
  waiting for transfers between devices  103 us (24%)
  blocking collectives  79.9 us (19%)
  other arithmetic  32.3 us (8%)
  local copies, waits for them, and re-layouts  30.7 us (7%)
  between operations  14 us (3%)
    psum x1, blocking collectives, body(): lax.psum((gain_q, gain_k + gain_kp), ('prompt', 'comp'))  79.9 us
    reduce_scatter x1, waiting for transfers between devices, body(): lax.psum_scatter(terms.astype(jnp.bfloat16), 'comp', scatter_dimension=0,...  43.3 us
    all_gather x1, waiting for transfers between devices, body(): lax.all_gather(v_prompt[0], 'comp', axis=0, tiled=True)  30.1 us
    all_gather x1, waiting for transfers between devices, body(): lax.all_gather(k_prompt[0], 'comp', axis=0, tiled=True)  28.3 us
    dot_general x8, matrix products, head_pass(): jnp.einsum('sgd,td->gst', g_head, pv_head, preferred_element_type=f32)  28.3 us
    dot_general x8, matrix products, head_pass(): jnp.einsum('gst,sgd->td', dsb_p, q_head, preferred_element_type=f32) * scale  19 us
    dot_general x8, matrix products, head_pass(): jnp.einsum('gst,td->sgd', probb_p, pv_head, preferred_element_type=f32)  16.6 us
    dot_general x8, matrix products, head_pass(): jnp.einsum('gst,td->sgd', dsb_c, ok_head, preferred_element_type=f32)  14.2 us
  transfers between devices with their start and end apart: 3, of which 3 were waited for; matrix products, arithmetic and copies ran while one was open for 9% of the time, Pallas kernels for 0%

commit v1 on v0

v1 whole, which is shorter than its diff:
```python
import functools
import math

import jax
import jax.numpy as jnp
from jax import lax
from jax.experimental import pallas as pl
from jax.experimental.pallas import tpu as pltpu
from jax.sharding import PartitionSpec as P

MESH = pl.DeviceIdType.MESH
f32 = jnp.float32
bf16 = jnp.bfloat16
KVH = 8
GRP = 8
HD = 128
SLOTS = 128
PL = 1024
KEYS = PL + SLOTS
ROWS = GRP * SLOTS
PAGE = 64
NZ = 8
NB = 16
CH = 256
TILE = 128
NT_ = KEYS // TILE
EPS = 1e-6
SCALE = 1.0 / math.sqrt(HD)
LOG2 = SCALE * math.log2(math.e)
FILL = 5
TICKS = FILL + KVH + 5

NT = (((1,), (1,)), ((), ()))
NN = (((1,), (0,)), ((), ()))


def dot(a, b, dims):
    return lax.dot_general(a, b, dims, preferred_element_type=f32)


def fold(x, op):
    return op(x.reshape(x.shape[0] // 8, 8, x.shape[1]), axis=0)


def cols(h, i=0, n=1):
    return pl.ds(pl.multiple_of(h * (n * HD) + i * HD, HD), HD)


def inv_rms(x):
    return lax.rsqrt(jnp.mean(x * x, axis=-1, keepdims=True) + EPS)


def norm_grad(x, gain, dy):
    r = inv_rms(x)
    xr = x * r
    u = dy * gain
    dx = r * (u - xr * jnp.mean(xr * u, axis=-1, keepdims=True))
    return dx, dy * xr


def remote(src, dst, send, recv, device):
    return pltpu.make_async_remote_copy(
        src_ref=src, dst_ref=dst, send_sem=send, recv_sem=recv, device_id=device, device_id_type=MESH
    )


def kernel(
    q_hbm, do_hbm, kp, vp, kc, vc, lens, qg, kg,
    dq_hbm, dkc, dvc, dkp, dvp, gains,
    qv, dov, dqv, qn, okn, vis, kvb, sc, dp, pb, ds, acc, sib, rsr, rss, gq, gk, gsend, grecv,
    q_sem, do_sem, dq_sem, ag_s, ag_b, ag_r, sl_s, sl_r, rs_s, rs_r, g_s, g_r,
):
    p = lax.axis_index("prompt")
    me = lax.axis_index("comp")
    z, c = me // 2, me % 2
    px, py = p // 4, p % 4
    zmod = lambda v: lax.rem(v + 2 * NZ, NZ)
    zdev = lambda v: {"comp": zmod(v) * 2 + c}
    sibling = {"comp": z * 2 + (1 - c)}
    mine = c * NZ + z
    theirs = (1 - c) * NZ
    stages = (
        [(1, c, sibling)],
        [(8, z, zdev(z + i)) for i in range(1, 8)],
        [(4, px, {"prompt": lax.rem(px + i, 4) * 4 + py}) for i in range(1, 4)],
        [(4, py, {"prompt": px * 4 + lax.rem(py + i, 4)}) for i in range(1, 4)],
    )

    barrier = pltpu.get_barrier_semaphore()
    for stage in stages:
        for _, _, dev in stage:
            pl.semaphore_signal(barrier, inc=1, device_id=dev, device_id_type=MESH)

    quarter = ROWS * 2
    for i in range(4):
        part = pl.ds(i * quarter, quarter)
        pltpu.make_async_copy(q_hbm.at[:, part], qv.at[:, part], q_sem.at[i]).start()
    pltpu.make_async_copy(do_hbm, dov, do_sem).start()

    for h in range(KVH):
        x = kp[:, h * HD : (h + 1) * HD].astype(f32)
        kvb[h, mine, 0] = (x * inv_rms(x) * kg[...]).astype(bf16)
        kvb[h, mine, 1] = vp[:, h * HD : (h + 1) * HD]
        x = kc[:, h * HD : (h + 1) * HD].astype(f32)
        okn[h] = (x * inv_rms(x) * kg[...]).astype(bf16)
    gq[...] = jnp.zeros_like(gq)
    gk[...] = jnp.zeros_like(gk)
    t_at = lax.broadcasted_iota(jnp.int32, (SLOTS, SLOTS), 0)
    s_at = lax.broadcasted_iota(jnp.int32, (SLOTS, SLOTS), 1)
    seg_t = jnp.zeros((SLOTS, SLOTS), jnp.int32)
    seg_s = jnp.zeros((SLOTS, SLOTS), jnp.int32)
    end = jnp.zeros((1, 1), jnp.int32)
    for i in range(4):
        end = end + lens[0:1, i : i + 1]
        seg_t += (t_at >= end).astype(jnp.int32)
        seg_s += (s_at >= end).astype(jnp.int32)
    seen = ((seg_t == seg_s) & (t_at <= s_at)).astype(f32)
    vis[...] = jnp.concatenate([seen] * (CH // SLOTS), axis=1)

    pl.semaphore_wait(barrier, sum(len(s) for s in stages))

    def between(v, lo, hi):
        return jnp.logical_and(v >= lo, v < hi)

    def block(h, slot, send, recv_slot_sem, dev):
        return remote(kvb.at[h, slot], kvb.at[h, slot], send, recv_slot_sem, dev)

    def gather(tick):
        h0 = tick

        @pl.when(between(h0, 0, KVH))
        def _():
            rsem = ag_r.at[h0, mine]
            block(h0, mine, ag_s.at[h0, 0, 0], rsem, zdev(z + 1)).start()
            block(h0, mine, ag_s.at[h0, 1, 0], rsem, zdev(z - 1)).start()
            block(h0, mine, ag_b.at[h0, 0], rsem, sibling).start()

        for k in (1, 2, 3):
            h = tick - k

            @pl.when(between(h, 0, KVH))
            def _(h=h, k=k):
                odd = lax.rem(h, 2)
                for d in (0, 1):
                    step = 1 - 2 * d
                    slot = c * NZ + zmod(z - step * k)
                    rsem = ag_r.at[h, slot]
                    block(h, slot, ag_b.at[h, 0], rsem, sibling).wait_recv()
                    if k < 3:
                        block(h, slot, ag_s.at[h, d, k], rsem, zdev(z + step)).start()
                    block(h, slot, ag_b.at[h, 1 + 3 * d + k - 1], rsem, sibling).start()
                if k == 3:
                    step = 1 - 2 * odd
                    slot = c * NZ + zmod(z - step * 3)
                    block(h, slot, ag_s.at[h, odd, 3], ag_r.at[h, slot], zdev(z + step)).start()

        h4 = tick - 4

        @pl.when(between(h4, 0, KVH))
        def _():
            slot = c * NZ + zmod(z + 4)
            rsem = ag_r.at[h4, slot]
            block(h4, slot, ag_b.at[h4, 7], rsem, sibling).wait_recv()
            block(h4, slot, ag_b.at[h4, 7], rsem, sibling).start()

    def prepare(h):
        for g in range(GRP):
            x = qv[:, cols(h, g, GRP)].astype(f32)
            qn[h, g * SLOTS : (g + 1) * SLOTS] = (x * inv_rms(x) * qg[...]).astype(bf16)

    def compute(h):
        for i in range(NZ):
            slot = theirs + i
            block(h, slot, ag_b.at[h, 0], ag_r.at[h, slot], sibling).wait_recv()

        def keys(t):
            return okn[h] if t == NT_ - 1 else kvb[h, 2 * t : 2 * t + 2, 0].reshape(TILE, HD)

        def vals(t):
            return vc[:, cols(h)] if t == NT_ - 1 else kvb[h, 2 * t : 2 * t + 2, 1].reshape(TILE, HD)

        grads = jnp.concatenate([dov[:, cols(h, g, GRP)] for g in range(GRP)], axis=0)
        for lo in range(0, ROWS, CH):
            at = slice(lo, lo + CH)
            qc = qn[h, at]
            gc = grads[at]
            top = None
            for t in range(NT_):
                ts = slice(t * TILE, (t + 1) * TILE)
                s = dot(keys(t), qc, NT)
                if t == NT_ - 1:
                    s = jnp.where(vis[...] > 0, s, -1e30)
                sc[ts, at] = s
                part = fold(s, jnp.max)
                top = part if top is None else jnp.maximum(top, part)
            top = jnp.max(top, axis=0, keepdims=True) * LOG2
            total = None
            for t in range(NT_):
                ts = slice(t * TILE, (t + 1) * TILE)
                e = jnp.exp2(sc[ts, at] * LOG2 - top)
                sc[ts, at] = e
                part = fold(e, jnp.sum)
                total = part if total is None else total + part
            inv = 1.0 / jnp.sum(total, axis=0, keepdims=True)
            delta = None
            for t in range(NT_):
                ts = slice(t * TILE, (t + 1) * TILE)
                d = dot(vals(t), gc, NT)
                dp[ts, at] = d
                b = (sc[ts, at] * inv).astype(bf16)
                pb[ts, at] = b
                part = fold(b.astype(f32) * d, jnp.sum)
                delta = part if delta is None else delta + part
            delta = jnp.sum(delta, axis=0, keepdims=True)
            for t in range(NT_):
                ts = slice(t * TILE, (t + 1) * TILE)
                ds[ts, at] = (sc[ts, at] * inv * (dp[ts, at] - delta)).astype(bf16)
        dv = dot(pb[...], grads, NN)
        dk = dot(ds[...], qn[h], NN) * SCALE
        gk_terms = jnp.zeros((8, HD), f32)
        for b in range(NB):
            rows = slice(b * PAGE, (b + 1) * PAGE)
            acc[h, b, 0] = dk[rows]
            acc[h, b, 1] = dv[rows]
            gk_terms += fold(dk[rows] * kvb[h, b, 0].astype(f32), jnp.sum)
        remote(
            acc.at[h, pl.ds(theirs, NZ)], sib.at[h], sl_s.at[h], sl_r.at[h], sibling
        ).start()
        dx, own_terms = norm_grad(kc[:, cols(h)].astype(f32), kg[...], dk[PL:])
        dkc[:, cols(h)] = dx.astype(bf16)
        dvc[:, cols(h)] = dv[PL:].astype(bf16)
        gk[...] += gk_terms / kg[...] + fold(own_terms, jnp.sum)
        kt = jnp.concatenate([keys(t).T for t in range(NT_)], axis=1)
        dqt = dot(kt, ds[...], NN)
        gq_terms = jnp.zeros((8, HD), f32)
        for g in range(GRP):
            dy = dqt[:, g * SLOTS : (g + 1) * SLOTS].T * SCALE
            at = cols(h, g, GRP)
            dx, terms = norm_grad(qv[:, at].astype(f32), qg[...], dy)
            gq_terms += fold(terms, jnp.sum)
            dqv[:, at] = dx.astype(bf16)
        gq[...] += gq_terms
        span = pl.ds(pl.multiple_of(h * ROWS, ROWS), ROWS)
        pltpu.make_async_copy(dqv.at[:, span], dq_hbm.at[:, span], dq_sem.at[h]).start()

    def hop(h, d, j):
        return remote(
            rss.at[h, d, j], rsr.at[h, d, j], rs_s.at[h, d, j], rs_r.at[h, d, j], zdev(z + 1 - 2 * d)
        )

    def chip_sum(h, t):
        return acc[h, c * NZ + t] + sib[h, t]

    def reduce(tick):
        for j in (1, 2, 3):
            h = tick - FILL - j

            @pl.when(between(h, 0, KVH))
            def _(h=h, j=j):
                odd = lax.rem(h, 2)
                if j == 1:
                    remote(sib.at[h], sib.at[h], sl_s.at[h], sl_r.at[h], sibling).wait_recv()
                for d in (0, 1):
                    length = 3 + (odd if d else 1 - odd)
                    val = chip_sum(h, zmod(z + (1 - 2 * d) * (length - j + 1)))
                    if j > 1:
                        hop(h, d, j - 2).wait_recv()
                        val = val + rsr[h, d, j - 2].astype(f32)
                    rss[h, d, j - 1] = val.astype(bf16)
                    hop(h, d, j - 1).start()

        h = tick - FILL - 4

        @pl.when(between(h, 0, KVH))
        def _():
            d = lax.rem(h, 2)
            hop(h, d, 2).wait_recv()
            val = chip_sum(h, zmod(z + 1 - 2 * d)) + rsr[h, d, 2].astype(f32)
            rss[h, d, 3] = val.astype(bf16)
            hop(h, d, 3).start()

        hf = tick - FILL - 5

        @pl.when(between(hf, 0, KVH))
        def _():
            d = lax.rem(hf, 2)
            hop(hf, d, 3).wait_recv()
            hop(hf, 1 - d, 2).wait_recv()
            val = chip_sum(hf, z) + (rsr[hf, d, 3].astype(f32) + rsr[hf, 1 - d, 2].astype(f32))
            dx, _ = norm_grad(kp[:, cols(hf)].astype(f32), kg[...], val[0])
            dkp[:, cols(hf)] = dx.astype(bf16)
            dvp[:, cols(hf)] = val[1].astype(bf16)

    base = (0, 2, 10, 14)

    def gain_copy(i, slot_of, src_dev, n):
        return remote(gsend.at[i], grecv.at[slot_of], g_s.at[i, n], g_r.at[slot_of], src_dev)

    def share_gains(i):
        index = stages[i][0][1]
        slot = base[i] + index
        grecv[slot] = gsend[i]
        for n, (_, _, dev) in enumerate(stages[i]):
            gain_copy(i, slot, dev, n).start()

    def sum_gains(i):
        index = stages[i][0][1]
        size = (2, 8, 4, 4)[i]
        for n in range(1, size):
            slot = base[i] + lax.rem(index + n, size)
            gain_copy(i, slot, stages[i][0][2], 0).wait_recv()
        total = grecv[base[i]]
        for n in range(1, size):
            total = total + grecv[base[i] + n]
        return total

    def step(tick, carry):
        gather(tick)
        reduce(tick)

        for i in range(4):

            @pl.when(tick == FILL + KVH + i)
            def _(i=i):
                if i == 0:
                    q_sum = jnp.sum(gq[...], axis=0, keepdims=True)
                    k_sum = jnp.sum(gk[...], axis=0, keepdims=True)
                    row = lax.broadcasted_iota(jnp.int32, (8, HD), 0)
                    gsend[0] = jnp.where(row == 0, q_sum, jnp.where(row == 1, k_sum, 0.0))
                else:
                    gsend[i] = sum_gains(i - 1)
                share_gains(i)

        @pl.when(tick < 4)
        def _():
            part = pl.ds(pl.multiple_of(tick * quarter, quarter), quarter)
            pltpu.make_async_copy(q_hbm.at[:, part], qv.at[:, part], q_sem.at[tick]).wait()
            prepare(2 * tick)
            prepare(2 * tick + 1)

        @pl.when(tick == 4)
        def _():
            pltpu.make_async_copy(do_hbm, dov, do_sem).wait()

        @pl.when(between(tick, FILL, FILL + KVH))
        def _():
            compute(tick - FILL)

        return carry

    lax.fori_loop(0, TICKS, step, 0)
    gains[...] = sum_gains(3)

    def drain(h, carry):
        odd = lax.rem(h, 2)
        for d in (0, 1):
            for k in range(3):
                block(h, mine, ag_s.at[h, d, k], ag_r.at[h, mine], sibling).wait_send()
                hop(h, d, k).wait_send()
        block(h, mine, ag_s.at[h, odd, 3], ag_r.at[h, mine], sibling).wait_send()
        hop(h, odd, 3).wait_send()
        for k in range(NZ):
            block(h, mine, ag_b.at[h, k], ag_r.at[h, mine], sibling).wait_send()
        remote(sib.at[h], sib.at[h], sl_s.at[h], sl_r.at[h], sibling).wait_send()
        span = pl.ds(pl.multiple_of(h * ROWS, ROWS), ROWS)
        pltpu.make_async_copy(dqv.at[:, span], dq_hbm.at[:, span], dq_sem.at[h]).wait()
        return carry

    lax.fori_loop(0, KVH, drain, 0)
    for i in range(4):
        for n, (_, _, dev) in enumerate(stages[i]):
            gain_copy(i, base[i], dev, n).wait_send()


def body(q_raw, d_out, k_prompt, v_prompt, k_comp, v_comp, lengths, q_gain, k_gain):
    vmem = pl.BlockSpec(memory_space=pltpu.VMEM)
    hbm = pl.BlockSpec(memory_space=pl.ANY)
    dma = pltpu.SemaphoreType.DMA
    wide = KVH * HD
    shape = jax.ShapeDtypeStruct
    outs = pl.pallas_call(
        kernel,
        out_shape=(
            shape((SLOTS, GRP * wide), bf16),
            shape((SLOTS, wide), bf16),
            shape((SLOTS, wide), bf16),
            shape((PAGE, wide), bf16),
            shape((PAGE, wide), bf16),
            shape((8, HD), f32),
        ),
        in_specs=[hbm, hbm] + [vmem] * 7,
        out_specs=[hbm] + [vmem] * 5,
        scratch_shapes=[
            pltpu.VMEM((SLOTS, GRP * wide), bf16),
            pltpu.VMEM((SLOTS, GRP * wide), bf16),
            pltpu.VMEM((SLOTS, GRP * wide), bf16),
            pltpu.VMEM((KVH, ROWS, HD), bf16),
            pltpu.VMEM((KVH, SLOTS, HD), bf16),
            pltpu.VMEM((SLOTS, CH), f32),
            pltpu.VMEM((KVH, NB, 2, PAGE, HD), bf16),
            pltpu.VMEM((KEYS, ROWS), f32),
            pltpu.VMEM((KEYS, ROWS), f32),
            pltpu.VMEM((KEYS, ROWS), bf16),
            pltpu.VMEM((KEYS, ROWS), bf16),
            pltpu.VMEM((KVH, NB, 2, PAGE, HD), f32),
            pltpu.VMEM((KVH, NZ, 2, PAGE, HD), f32),
            pltpu.VMEM((KVH, 2, 4, 2, PAGE, HD), bf16),
            pltpu.VMEM((KVH, 2, 4, 2, PAGE, HD), bf16),
            pltpu.VMEM((8, HD), f32),
            pltpu.VMEM((8, HD), f32),
            pltpu.VMEM((4, 8, HD), f32),
            pltpu.VMEM((18, 8, HD), f32),
            dma((4,)),
            dma(()),
            dma((KVH,)),
            dma((KVH, 2, 4)),
            dma((KVH, 8)),
            dma((KVH, NB)),
            dma((KVH,)),
            dma((KVH,)),
            dma((KVH, 2, 4)),
            dma((KVH, 2, 4)),
            dma((4, 8)),
            dma((18,)),
        ],
        compiler_params=pltpu.CompilerParams(
            collective_id=0, has_side_effects=True, vmem_limit_bytes=58 * 2**20
        ),
        cost_estimate=pl.CostEstimate(flops=13 * 10**9, bytes_accessed=8 * 2**20, transcendentals=10**7),
        name="attention_backward",
    )(
        q_raw[0], d_out[0], k_prompt[0], v_prompt[0], k_comp[0], v_comp[0], lengths[0],
        q_gain.reshape(1, HD), k_gain.reshape(1, HD),
    )
    dq, dk_own, dv_own, dk_page, dv_page, gains = outs
    return dq[None], dk_own[None], dv_own[None], dk_page[None], dv_page[None], gains[0], gains[1]


def solution(mesh):
    split = P("prompt", "comp", None)
    return jax.shard_map(
        body,
        mesh=mesh,
        in_specs=(split,) * 7 + (P(), P()),
        out_specs=(split,) * 5 + (P(), P()),
        check_vma=False,
    )
```

time: 427 us -> 106 us (0.25)
  matrix products: 162 us -> 0 us
  waiting for transfers between devices: 103 us -> 0 us
  Pallas kernels: 0 us -> 96.5 us
  blocking collectives: 79.9 us -> 0 us
  other arithmetic: 32.3 us -> 0 us
  local copies, waits for them, and re-layouts: 30.7 us -> 7.16 us
  between operations: 14 us -> 0.66 us
    dot_general x96 -> x0, matrix products: 162 us -> none  [the longest x8 28.3 us: head_pass(): jnp.einsum('sgd,td->gst', g_head, pv_head, preferred_element_type=f32)]
    pallas_call x0 -> x1, Pallas kernels: none -> 96.5 us  [body(): pl.pallas_call(kernel, out_shape=(shape((SLOTS, GRP * wide), bf16), shape...]
    psum x1 -> x0, blocking collectives: 79.9 us -> none  [body(): lax.psum((gain_q, gain_k + gain_kp), ('prompt', 'comp'))]
    all_gather x2 -> x0, waiting for transfers between devices: 58.4 us -> none  [the longest x1 30.1 us: body(): lax.all_gather(v_prompt[0], 'comp', axis=0, tiled=True)]
    reduce_scatter x1 -> x0, waiting for transfers between devices: 43.3 us -> none  [body(): lax.psum_scatter(terms.astype(jnp.bfloat16), 'comp', scatter_dimension=0,...]
    reduce_sum x24 -> x0, other arithmetic: 18 us -> none  [the longest x3 6.19 us: norm_back(): jnp.sum((grad * values * inverse).reshape(-1, values.shape[-1]), axis=0)]
    convert_element_type x5 -> x0, local copies, waits for them, and re-layouts: 8.24 us -> none  [the longest x2 4.35 us: norm_rows(): values = values.astype(jnp.float32)]
    all_gather x2 -> x0, local copies, waits for them, and re-layouts: 7.92 us -> none  [the longest x1 3.96 us: body(): lax.all_gather(k_prompt[0], 'comp', axis=0, tiled=True)]
  transfers between devices with their start and end apart: 3 -> 0, of which waited for: 3 -> 0; matrix products, arithmetic and copies ran while one was open for 9% -> 0% of each run, Pallas kernels for 0% -> 0%
where the time goes in v1:
time: 106 us; the launch traced here: 104 us
  Pallas kernels  96.5 us (91%)
  local copies, waits for them, and re-layouts  7.16 us (7%)
    pallas_call x1, Pallas kernels, body(): pl.pallas_call(kernel, out_shape=(shape((SLOTS, GRP * wide), bf16), shape...  96.5 us
    unnamed x13, local copies, waits for them, and re-layouts  5.9 us

profile of v1, /device:TPU:1, one launch (start us, length us, event | category | flops | bytes accessed | tf_op | source)
XLA Modules:
  0.0 104.3 jit_solution(15553776244360981187)
XLA Ops:
  0.6 96.5 %attention_backward.1 = (bf16[128,8192]{1,0:T(8,128)(2,1)}, bf16[128,1024]{1,0:T(8,128)(2,1)}, bf16[128,1024]{1,0:T(8,128)(2,1)}, bf16[64,1024]{1,0:T(8,128)(2,1...) custom-call(bf16[128,8192]{1,0:T(8,128)(2,1)} %bitcast.23, bf16[128,8192]{1,0:T(8,128)(2,1)} %bitcast.24, ...), custom_call_target="tpu_custom_call" | custom-call | flops 12999999488 | bytes 8388608 | tf_op jit(solution)/shard_map/attention_backward/pallas_call | solution.py:381
  97.1 1.3 %slice_bitcast_fusion = (f32[128]{0:T(128)}, f32[128]{0:T(128)}) fusion(f32[8,128]{1,0:T(8,128)} %get-tuple-element.18), kind=kLoop, calls=%fused_computation | loop fusion | bytes 2048 | tf_op jit(solution)/shard_map/squeeze | solution.py:436
  98.4 0.0 copy-start.1
  98.4 0.0 copy-start
  98.4 0.0 copy-start.3
  98.4 0.0 copy-start.2
  98.4 3.2 %copy.21 = bf16[1,128,8192]{2,1,0:T(8,128)(2,1)} copy(bf16[1,128,8192]{2,1,0:T(8,128)(2,1)} %bitcast.18) | data formatting | bytes 4194304
  101.5 0.0 copy-done.1
  101.6 0.7 copy.22
  102.3 0.0 copy-done
  102.3 0.7 copy.23
  103.0 0.0 copy-done.3
  103.0 0.7 copy.24
  103.6 0.0 copy-done.2
  103.6 0.7 copy.25
Async XLA Ops:
  98.4 3.2 %copy-start.1 = (bf16[128,1024]{1,0:T(8,128)(2,1)S(1)}, bf16[128,1024]{1,0:T(8,128)(2,1)}, u32[]{:S(2)}) copy-start(bf16[128,1024]{1,0:T(8,128)(2,1)} %get-tuple-element.14) | copy-start | bytes 786436
  98.4 3.9 %copy-start = (bf16[128,1024]{1,0:T(8,128)(2,1)S(1)}, bf16[128,1024]{1,0:T(8,128)(2,1)}, u32[]{:S(2)}) copy-start(bf16[128,1024]{1,0:T(8,128)(2,1)} %get-tuple-element.15) | copy-start | bytes 786436
  98.4 4.6 %copy-start.3 = (bf16[64,1024]{1,0:T(8,128)(2,1)S(1)}, bf16[64,1024]{1,0:T(8,128)(2,1)}, u32[]{:S(2)}) copy-start(bf16[64,1024]{1,0:T(8,128)(2,1)} %get-tuple-element.16) | copy-start | bytes 393220
  98.4 5.2 %copy-start.2 = (bf16[64,1024]{1,0:T(8,128)(2,1)S(1)}, bf16[64,1024]{1,0:T(8,128)(2,1)}, u32[]{:S(2)}) copy-start(bf16[64,1024]{1,0:T(8,128)(2,1)} %get-tuple-element.17) | copy-start | bytes 393220

commit v2 on v1

v2 whole, which is shorter than its diff:
```python
import functools
import math

import jax
import jax.numpy as jnp
from jax import lax
from jax.experimental import pallas as pl
from jax.experimental.pallas import tpu as pltpu
from jax.sharding import PartitionSpec as P

MESH = pl.DeviceIdType.MESH
f32 = jnp.float32
bf16 = jnp.bfloat16
KVH = 8
GRP = 8
HD = 128
SLOTS = 128
PL = 1024
KEYS = PL + SLOTS
ROWS = GRP * SLOTS
PAGE = 64
NZ = 8
NB = 16
CH = 256
TILE = 128
NT_ = KEYS // TILE
EPS = 1e-6
SCALE = 1.0 / math.sqrt(HD)
LOG2 = SCALE * math.log2(math.e)
HALF = ROWS // 2

NT = (((1,), (1,)), ((), ()))
NN = (((1,), (0,)), ((), ()))


def dot(a, b, dims):
    return lax.dot_general(a, b, dims, preferred_element_type=f32)


def fold(x, op):
    return op(x.reshape(x.shape[0] // 8, 8, x.shape[1]), axis=0)


def cols(h, i=0, n=1):
    return pl.ds(pl.multiple_of(h * (n * HD) + i * HD, HD), HD)


def inv_rms(x):
    return lax.rsqrt(jnp.mean(x * x, axis=-1, keepdims=True) + EPS)


def norm_grad(x, gain, dy):
    r = inv_rms(x)
    xr = x * r
    u = dy * gain
    dx = r * (u - xr * jnp.mean(xr * u, axis=-1, keepdims=True))
    return dx, dy * xr


def remote(src, dst, send, recv, device):
    return pltpu.make_async_remote_copy(
        src_ref=src, dst_ref=dst, send_sem=send, recv_sem=recv, device_id=device, device_id_type=MESH
    )


def kernel(
    q_hbm, do_hbm, kp, vp, kc, vc, lens, qg, kg,
    dq_hbm, dkc, dvc, dkp, dvp, gq_out, gk_out,
    qv, dov, qn, okn, vis, kvb, sc, dp, pb, ds, pdv, pdk, acc, sib, rsr, rss, gq, gk, gsend, grecv,
    q_sem, do_sem, dq_sem, ag_s, ag_b, ag_r, ag_v, sl_s, sl_r, rs_s, rs_r, g_s, g_r,
):
    p = lax.axis_index("prompt")
    me = lax.axis_index("comp")
    z, c = me // 2, me % 2
    px, py = p // 4, p % 4
    zmod = lambda v: lax.rem(v + 2 * NZ, NZ)
    zdev = lambda v: {"comp": zmod(v) * 2 + c}
    sibling = {"comp": z * 2 + (1 - c)}
    mine = c * NZ + z
    theirs = (1 - c) * NZ
    stages = (
        [(1, c, sibling)],
        [(8, z, zdev(z + i)) for i in range(1, 8)],
        [(4, px, {"prompt": lax.rem(px + i, 4) * 4 + py}) for i in range(1, 4)],
        [(4, py, {"prompt": px * 4 + lax.rem(py + i, 4)}) for i in range(1, 4)],
    )

    barrier = pltpu.get_barrier_semaphore()
    for stage in stages:
        for _, _, dev in stage:
            pl.semaphore_signal(barrier, inc=1, device_id=dev, device_id_type=MESH)

    quarter = ROWS * 2
    for i in range(4):
        part = pl.ds(i * quarter, quarter)
        pltpu.make_async_copy(q_hbm.at[:, part], qv.at[:, part], q_sem.at[i]).start()
    pltpu.make_async_copy(do_hbm, dov, do_sem).start()

    for h in range(KVH):
        x = kp[:, h * HD : (h + 1) * HD].astype(f32)
        kvb[h, mine, 0] = (x * inv_rms(x) * kg[...]).astype(bf16)
        kvb[h, mine, 1] = vp[:, h * HD : (h + 1) * HD]
        x = kc[:, h * HD : (h + 1) * HD].astype(f32)
        okn[h] = (x * inv_rms(x) * kg[...]).astype(bf16)
    gq[...] = jnp.zeros_like(gq)
    gk[...] = jnp.zeros_like(gk)
    t_at = lax.broadcasted_iota(jnp.int32, (SLOTS, SLOTS), 0)
    s_at = lax.broadcasted_iota(jnp.int32, (SLOTS, SLOTS), 1)
    seg_t = jnp.zeros((SLOTS, SLOTS), jnp.int32)
    seg_s = jnp.zeros((SLOTS, SLOTS), jnp.int32)
    end = jnp.zeros((1, 1), jnp.int32)
    for i in range(4):
        end = end + lens[0:1, i : i + 1]
        seg_t += (t_at >= end).astype(jnp.int32)
        seg_s += (s_at >= end).astype(jnp.int32)
    seen = ((seg_t == seg_s) & (t_at <= s_at)).astype(f32)
    vis[...] = jnp.concatenate([seen] * (CH // SLOTS), axis=1)

    pl.semaphore_wait(barrier, sum(len(s) for s in stages))

    def between(v, lo, hi):
        return jnp.logical_and(v >= lo, v < hi)

    def block(h, slot, send, recv_slot_sem, dev):
        return remote(kvb.at[h, slot], kvb.at[h, slot], send, recv_slot_sem, dev)

    def arrived(h, slot):
        block(h, slot, ag_b.at[h, 0], ag_r.at[h, slot], sibling).wait_recv()

    def half_block(h, slot, n, send, recv, dev):
        return remote(kvb.at[h, slot, n], kvb.at[h, slot, n], send, recv, dev)

    def forward(h, slot, n):
        block(h, slot, ag_b.at[h, n], ag_r.at[h, slot], sibling).start()

    def gather_near(h):
        @pl.when(between(h, 0, KVH))
        def _():
            for n, i in enumerate((2, -2, 1, -1)):
                block(h, mine, ag_s.at[h, n], ag_r.at[h, mine], zdev(z + i)).start()
            forward(h, mine, 0)

    def gather_far(h):
        @pl.when(between(h, 0, KVH))
        def _():
            for n, step in enumerate((1, -1)):
                slot = c * NZ + zmod(z - 2 * step)
                arrived(h, slot)
                block(h, slot, ag_s.at[h, 4 + n], ag_r.at[h, slot], zdev(z + step)).start()
                recv = ag_v.at[h] if n else ag_r.at[h, slot]
                half_block(h, slot, n, ag_s.at[h, 6 + n], recv, zdev(z + 2 * step)).start()
                forward(h, slot, 1 + n)
            for n, step in enumerate((1, -1)):
                slot = c * NZ + zmod(z - step)
                arrived(h, slot)
                forward(h, slot, 3 + n)

    def gather_end(h, low):
        @pl.when(between(h, low, KVH))
        def _():
            for n, step in enumerate((1, -1)):
                slot = c * NZ + zmod(z - 3 * step)
                arrived(h, slot)
                forward(h, slot, 5 + n)
            slot = c * NZ + zmod(z + 4)
            half_block(h, slot, 0, ag_s.at[h, 6], ag_r.at[h, slot], sibling).wait_recv()
            half_block(h, slot, 1, ag_s.at[h, 7], ag_v.at[h], sibling).wait_recv()
            forward(h, slot, 7)

    def prepare(h):
        for g in range(GRP):
            x = qv[:, cols(h, g, GRP)].astype(f32)
            y = x * inv_rms(x) * qg[...]
            near = y.astype(bf16)
            at = slice(g * SLOTS, (g + 1) * SLOTS)
            qn[h, at, :HD] = near
            qn[h, at, HD:] = (y - near.astype(f32)).astype(bf16)

    def keys(h, t):
        return okn[h] if t == NT_ - 1 else kvb[h, 2 * t : 2 * t + 2, 0].reshape(TILE, HD)

    def vals(h, t):
        return vc[:, cols(h)] if t == NT_ - 1 else kvb[h, 2 * t : 2 * t + 2, 1].reshape(TILE, HD)

    def soft(h, half):
        heads = range(half * GRP // 2, (half + 1) * GRP // 2)
        grads = jnp.concatenate([dov[:, cols(h, g, GRP)] for g in heads], axis=0)
        for n, lo in enumerate(range(half * HALF, (half + 1) * HALF, CH)):
            at = slice(lo, lo + CH)
            own = slice(lo - half * HALF, lo - half * HALF + CH)
            qc = qn[h, at, :HD]
            gc = grads[own]
            top = None
            for t in range(NT_):
                ts = slice(t * TILE, (t + 1) * TILE)
                s = dot(keys(h, t), qc, NT)
                if t == NT_ - 1:
                    s = jnp.where(vis[...] > 0, s, -1e30)
                sc[n, ts] = s
                part = fold(s, jnp.max)
                top = part if top is None else jnp.maximum(top, part)
            top = jnp.max(top, axis=0, keepdims=True) * LOG2
            total = None
            for t in range(NT_):
                ts = slice(t * TILE, (t + 1) * TILE)
                e = jnp.exp2(sc[n, ts] * LOG2 - top)
                sc[n, ts] = e
                part = fold(e, jnp.sum)
                total = part if total is None else total + part
            inv = 1.0 / jnp.sum(total, axis=0, keepdims=True)
            delta = None
            for t in range(NT_):
                ts = slice(t * TILE, (t + 1) * TILE)
                d = dot(vals(h, t), gc, NT)
                dp[n, ts] = d
                b = (sc[n, ts] * inv).astype(bf16)
                pb[ts, own] = b
                part = fold(b.astype(f32) * d, jnp.sum)
                delta = part if delta is None else delta + part
            delta = jnp.sum(delta, axis=0, keepdims=True)
            for t in range(NT_):
                ts = slice(t * TILE, (t + 1) * TILE)
                ds[h, ts, at] = (sc[n, ts] * inv * (dp[n, ts] - delta)).astype(bf16)
        at = slice(half * HALF, (half + 1) * HALF)
        return dot(pb[...], grads, NN), dot(ds[h, :, at], qn[h, at], NN)

    def compute(h, between_halves):
        for i in range(NZ):
            arrived(h, theirs + i)
        dv, dk = soft(h, 0)
        pdv[...] = dv
        pdk[...] = dk
        between_halves()
        dv, dk = soft(h, 1)
        dv = dv + pdv[...]
        both = (dk + pdk[...]) * SCALE
        dk = both[:, :HD]
        exact = dk + both[:, HD:]
        gk_terms = jnp.zeros((8, HD), f32)
        gq_terms = fold(exact[PL:] * okn[h].astype(f32), jnp.sum)
        for b in range(NB):
            rows = slice(b * PAGE, (b + 1) * PAGE)
            acc[h, b, 0] = dk[rows]
            acc[h, b, 1] = dv[rows]
            key = kvb[h, b, 0].astype(f32)
            gk_terms += fold(dk[rows] * key, jnp.sum)
            gq_terms += fold(exact[rows] * key, jnp.sum)
        remote(
            acc.at[h, pl.ds(theirs, NZ)], sib.at[h], sl_s.at[h], sl_r.at[h], sibling
        ).start()
        dx, own_terms = norm_grad(kc[:, cols(h)].astype(f32), kg[...], dk[PL:])
        dkc[:, cols(h)] = dx.astype(bf16)
        dvc[:, cols(h)] = dv[PL:].astype(bf16)
        gk[...] += gk_terms / kg[...] + fold(own_terms, jnp.sum)
        gq[...] += gq_terms / qg[...]

    def queries(h):
        kt = jnp.concatenate([keys(h, t).T for t in range(NT_)], axis=1)
        dqt = dot(kt, ds[h], NN)
        for g in range(GRP):
            dy = dqt[:, g * SLOTS : (g + 1) * SLOTS].T * SCALE
            at = cols(h, g, GRP)
            dx, _ = norm_grad(qv[:, at].astype(f32), qg[...], dy)
            qv[:, at] = dx.astype(bf16)
        dq_copy(h).start()

    def dq_copy(h):
        span = pl.ds(pl.multiple_of(h * ROWS, ROWS), ROWS)
        return pltpu.make_async_copy(qv.at[:, span], dq_hbm.at[:, span], dq_sem.at[h])

    def hop(h, d, j):
        return remote(
            rss.at[h, d, j], rsr.at[h, d, j], rs_s.at[h, d, j], rs_r.at[h, d, j], zdev(z + 1 - 2 * d)
        )

    def chip_sum(h, t):
        return acc[h, c * NZ + t] + sib[h, t]

    def reduce_hop(h, j):
        @pl.when(between(h, 0, KVH))
        def _():
            odd = lax.rem(h, 2)
            if j == 4:
                hop(h, odd, 2).wait_recv()
                val = chip_sum(h, zmod(z + 1 - 2 * odd)) + rsr[h, odd, 2].astype(f32)
                rss[h, odd, 3] = val.astype(bf16)
                hop(h, odd, 3).start()
                return
            if j == 1:
                remote(sib.at[h], sib.at[h], sl_s.at[h], sl_r.at[h], sibling).wait_recv()
            for d in (0, 1):
                length = 3 + (odd if d else 1 - odd)
                val = chip_sum(h, zmod(z + (1 - 2 * d) * (length - j + 1)))
                if j > 1:
                    hop(h, d, j - 2).wait_recv()
                    val = val + rsr[h, d, j - 2].astype(f32)
                rss[h, d, j - 1] = val.astype(bf16)
                hop(h, d, j - 1).start()

    def reduce_end(h):
        @pl.when(between(h, 0, KVH))
        def _():
            d = lax.rem(h, 2)
            hop(h, d, 3).wait_recv()
            hop(h, 1 - d, 2).wait_recv()
            val = chip_sum(h, z) + (rsr[h, d, 3].astype(f32) + rsr[h, 1 - d, 2].astype(f32))
            dx, _ = norm_grad(kp[:, cols(h)].astype(f32), kg[...], val[0])
            dkp[:, cols(h)] = dx.astype(bf16)
            dvp[:, cols(h)] = val[1].astype(bf16)

    def reduce(i):
        for j in (4, 3, 2, 1):
            reduce_hop(i - j, j)
        reduce_end(i - 5)

    base = (0, 2, 10, 14)

    def gain_copy(i, slot_of, src_dev, n):
        return remote(gsend.at[i], grecv.at[slot_of], g_s.at[i, n], g_r.at[slot_of], src_dev)

    def share_gains(i):
        index = stages[i][0][1]
        slot = base[i] + index
        grecv[slot] = gsend[i]
        for n, (_, _, dev) in enumerate(stages[i]):
            gain_copy(i, slot, dev, n).start()

    def sum_gains(i):
        index = stages[i][0][1]
        size = (2, 8, 4, 4)[i]
        for n in range(1, size):
            slot = base[i] + lax.rem(index + n, size)
            gain_copy(i, slot, stages[i][0][2], 0).wait_recv()
        total = grecv[base[i]]
        for n in range(1, size):
            total = total + grecv[base[i] + n]
        return total

    gather_near(0)
    gather_near(1)

    def fill(n, carry):
        part = pl.ds(pl.multiple_of(n * quarter, quarter), quarter)
        pltpu.make_async_copy(q_hbm.at[:, part], qv.at[:, part], q_sem.at[n]).wait()
        prepare(2 * n)
        prepare(2 * n + 1)

        @pl.when(n >= 2)
        def _():
            gather_far(n - 2)

        return carry

    lax.fori_loop(0, 4, fill, 0)
    gather_near(2)
    pltpu.make_async_copy(do_hbm, dov, do_sem).wait()
    gather_end(0, 0)

    def main(i, carry):
        gather_end(i + 1, 2)
        gather_far(i + 2)
        gather_near(i + 3)

        def between_halves():
            @pl.when(i == 0)
            def _():
                gather_end(1, 1)

            reduce(i)

        compute(i, between_halves)
        return carry

    lax.fori_loop(0, KVH, main, 0)

    def gain_step(i):
        if i == 0:
            q_sum = jnp.sum(gq[...], axis=0, keepdims=True)
            k_sum = jnp.sum(gk[...], axis=0, keepdims=True)
            row = lax.broadcasted_iota(jnp.int32, (8, HD), 0)
            gsend[0] = jnp.where(row == 0, q_sum, jnp.where(row == 1, k_sum, 0.0))
        else:
            gsend[i] = sum_gains(i - 1)
        share_gains(i)

    def late(n, carry):
        for i in range(4):

            @pl.when(n == i)
            def _(i=i):
                gain_step(i)

        @pl.when(n < 4)
        def _():
            queries(2 * n)

        reduce(KVH + n)

        @pl.when(n < 4)
        def _():
            queries(2 * n + 1)

        return carry

    lax.fori_loop(0, 5, late, 0)
    total = sum_gains(3)
    gq_out[...] = total[0:1]
    gk_out[...] = total[1:2]

    def drain(h, carry):
        odd = lax.rem(h, 2)
        for d in (0, 1):
            for k in range(3):
                hop(h, d, k).wait_send()
        hop(h, odd, 3).wait_send()

        for k in range(6):
            block(h, mine, ag_s.at[h, k], ag_r.at[h, mine], sibling).wait_send()
        for k in (0, 1):
            half_block(h, mine, k, ag_s.at[h, 6 + k], ag_v.at[h], sibling).wait_send()
        for k in range(NZ):
            block(h, mine, ag_b.at[h, k], ag_r.at[h, mine], sibling).wait_send()
        remote(sib.at[h], sib.at[h], sl_s.at[h], sl_r.at[h], sibling).wait_send()
        dq_copy(h).wait()
        return carry

    lax.fori_loop(0, KVH, drain, 0)
    for i in range(4):
        for n, (_, _, dev) in enumerate(stages[i]):
            gain_copy(i, base[i], dev, n).wait_send()


def body(q_raw, d_out, k_prompt, v_prompt, k_comp, v_comp, lengths, q_gain, k_gain):
    vmem = pl.BlockSpec(memory_space=pltpu.VMEM)
    hbm = pl.BlockSpec(memory_space=pl.ANY)
    dma = pltpu.SemaphoreType.DMA
    wide = KVH * HD
    shape = jax.ShapeDtypeStruct
    outs = pl.pallas_call(
        kernel,
        out_shape=(
            shape((SLOTS, GRP * wide), bf16),
            shape((SLOTS, wide), bf16),
            shape((SLOTS, wide), bf16),
            shape((PAGE, wide), bf16),
            shape((PAGE, wide), bf16),
            shape((1, HD), f32),
            shape((1, HD), f32),
        ),
        in_specs=[hbm, hbm] + [vmem] * 7,
        out_specs=[hbm] + [vmem] * 6,
        scratch_shapes=[
            pltpu.VMEM((SLOTS, GRP * wide), bf16),
            pltpu.VMEM((SLOTS, GRP * wide), bf16),
            pltpu.VMEM((KVH, ROWS, 2 * HD), bf16),
            pltpu.VMEM((KVH, SLOTS, HD), bf16),
            pltpu.VMEM((SLOTS, CH), f32),
            pltpu.VMEM((KVH, NB, 2, PAGE, HD), bf16),
            pltpu.VMEM((2, KEYS, CH), f32),
            pltpu.VMEM((2, KEYS, CH), f32),
            pltpu.VMEM((KEYS, HALF), bf16),
            pltpu.VMEM((KVH, KEYS, ROWS), bf16),
            pltpu.VMEM((KEYS, HD), f32),
            pltpu.VMEM((KEYS, 2 * HD), f32),
            pltpu.VMEM((KVH, NB, 2, PAGE, HD), f32),
            pltpu.VMEM((KVH, NZ, 2, PAGE, HD), f32),
            pltpu.VMEM((KVH, 2, 4, 2, PAGE, HD), bf16),
            pltpu.VMEM((KVH, 2, 4, 2, PAGE, HD), bf16),
            pltpu.VMEM((8, HD), f32),
            pltpu.VMEM((8, HD), f32),
            pltpu.VMEM((4, 8, HD), f32),
            pltpu.VMEM((18, 8, HD), f32),
            dma((4,)),
            dma(()),
            dma((KVH,)),
            dma((KVH, 8)),
            dma((KVH, 8)),
            dma((KVH, NB)),
            dma((KVH,)),
            dma((KVH,)),
            dma((KVH,)),
            dma((KVH, 2, 4)),
            dma((KVH, 2, 4)),
            dma((4, 8)),
            dma((18,)),
        ],
        compiler_params=pltpu.CompilerParams(
            collective_id=0, has_side_effects=True, vmem_limit_bytes=60 * 2**20
        ),
        cost_estimate=pl.CostEstimate(flops=13 * 10**9, bytes_accessed=8 * 2**20, transcendentals=10**7),
        name="attention_backward",
    )(
        q_raw[0], d_out[0], k_prompt[0], v_prompt[0], k_comp[0], v_comp[0], lengths[0],
        q_gain.reshape(1, HD), k_gain.reshape(1, HD),
    )
    *large, gq, gk = finish(outs)
    return tuple(x[None] for x in large) + (gq.reshape(HD), gk.reshape(HD))


def finish_kernel(*refs):
    ins, outs, stage, sem_in, sem_out = refs[:7], refs[7:14], refs[14:19], refs[19], refs[20]
    pieces = [(0, pl.ds(i * (SLOTS // 4), SLOTS // 4)) for i in range(4)]
    pieces += [(i, pl.ds(0, ins[i].shape[0])) for i in range(1, 5)]
    loads = [pltpu.make_async_copy(ins[i].at[at], stage[i].at[at], sem_in.at[n]) for n, (i, at) in enumerate(pieces)]
    stores = [pltpu.make_async_copy(stage[i].at[at], outs[i].at[at], sem_out.at[n]) for n, (i, at) in enumerate(pieces)]
    for copy in loads:
        copy.start()
    outs[5][...] = ins[5][...]
    outs[6][...] = ins[6][...]
    for load, store in zip(loads, stores):
        load.wait()
        store.start()
    for copy in stores:
        copy.wait()


def finish(arrays):
    vmem = pl.BlockSpec(memory_space=pltpu.VMEM)
    hbm = pl.BlockSpec(memory_space=pl.ANY)
    return pl.pallas_call(
        finish_kernel,
        out_shape=[jax.ShapeDtypeStruct(x.shape, x.dtype) for x in arrays],
        in_specs=[hbm] * 5 + [vmem] * 2,
        out_specs=[hbm] * 5 + [vmem] * 2,
        scratch_shapes=[pltpu.VMEM(x.shape, x.dtype) for x in arrays[:5]]
        + [pltpu.SemaphoreType.DMA((8,)), pltpu.SemaphoreType.DMA((8,))],
        name="finish",
    )(*arrays)


def solution(mesh):
    split = P("prompt", "comp", None)
    return jax.shard_map(
        body,
        mesh=mesh,
        in_specs=(split,) * 7 + (P(), P()),
        out_specs=(split,) * 5 + (P(), P()),
        check_vma=False,
    )
```

time: 106 us -> 94.1 us (0.89); the launches traced: 104 us -> 94 us
  local copies, waits for them, and re-layouts: 7.16 us -> 0 us
  Pallas kernels: 96.5 us -> 93.3 us
    pallas_call x1, Pallas kernels: 96.5 us -> 89.4 us  [body(): pl.pallas_call(kernel, out_shape=(shape((SLOTS, GRP * wide), bf16), shape...]
    unnamed x13 -> x0, local copies, waits for them, and re-layouts: 5.9 us -> none
    pallas_call x0 -> x1, Pallas kernels: none -> 3.92 us  [finish(): pl.pallas_call(finish_kernel, out_shape=[jax.ShapeDtypeStruct(x.shape, x....]
    squeeze x1 -> x0, local copies, waits for them, and re-layouts: 1.27 us -> none  [body(): gains[1]]
where the time goes in v2:
time: 94.1 us; the launch traced here: 94 us
  Pallas kernels  93.3 us (99%)
    pallas_call x1, Pallas kernels, body(): pl.pallas_call(kernel, out_shape=(shape((SLOTS, GRP * wide), bf16), shape...  89.4 us
    pallas_call x1, Pallas kernels, finish(): pl.pallas_call(finish_kernel, out_shape=[jax.ShapeDtypeStruct(x.shape, x....  3.92 us

profile of v2, /device:TPU:1, one launch (start us, length us, event | category | flops | bytes accessed | tf_op | source)
XLA Modules:
  0.0 94.0 jit_solution(13321790166235688838)
XLA Ops:
  0.6 89.4 %attention_backward.1 = (bf16[128,8192]{1,0:T(8,128)(2,1)}, bf16[128,1024]{1,0:T(8,128)(2,1)}, bf16[128,1024]{1,0:T(8,128)(2,1)}, bf16[64,1024]{1,0:T(8,128)(2,1...) custom-call(bf16[128,8192]{1,0:T(8,128)(2,1)} %bitcast.16, bf16[128,8192]{1,0:T(8,128)(2,1)} %bitcast.17, ...), custom_call_target="tpu_custom_call" | custom-call | flops 12999999488 | bytes 8388608 | tf_op jit(solution)/shard_map/attention_backward/pallas_call | solution.py:439
  90.0 3.9 %finish.1 = (bf16[128,8192]{1,0:T(8,128)(2,1)}, bf16[128,1024]{1,0:T(8,128)(2,1)}, bf16[128,1024]{1,0:T(8,128)(2,1)}, bf16[64,1024]{1,0:T(8,128)(2,1)}, bf16[64,...) custom-call(bf16[128,8192]{1,0:T(8,128)(2,1)} %get-tuple-element.21.refs_0_, ...), custom_call_target="tpu_custom_call" | custom-call | tf_op jit(solution)/shard_map/finish/pallas_call | solution.py:520

commit v3 on v2

--- a/solution.py
+++ b/solution.py
@@ -28,6 +28,7 @@
 SCALE = 1.0 / math.sqrt(HD)
 LOG2 = SCALE * math.log2(math.e)
 HALF = ROWS // 2
+EARLY = 3
 
 NT = (((1,), (1,)), ((), ()))
 NN = (((1,), (0,)), ((), ()))
@@ -66,7 +67,7 @@
 def kernel(
     q_hbm, do_hbm, kp, vp, kc, vc, lens, qg, kg,
     dq_hbm, dkc, dvc, dkp, dvp, gq_out, gk_out,
-    qv, dov, qn, okn, vis, kvb, sc, dp, pb, ds, pdv, pdk, acc, sib, rsr, rss, gq, gk, gsend, grecv,
+    qv, dov, qn, okn, qgt, vis, kvb, sc, dp, pb, ds, pdv, pdk, acc, slab, sib, rsr, rss, gq, gk, gsend, grecv,
     q_sem, do_sem, dq_sem, ag_s, ag_b, ag_r, ag_v, sl_s, sl_r, rs_s, rs_r, g_s, g_r,
 ):
     p = lax.axis_index("prompt")
@@ -102,6 +103,7 @@
         kvb[h, mine, 1] = vp[:, h * HD : (h + 1) * HD]
         x = kc[:, h * HD : (h + 1) * HD].astype(f32)
         okn[h] = (x * inv_rms(x) * kg[...]).astype(bf16)
+    qgt[...] = jnp.broadcast_to(qg[...] * SCALE, (SLOTS, HD)).T
     gq[...] = jnp.zeros_like(gq)
     gk[...] = jnp.zeros_like(gk)
     t_at = lax.broadcasted_iota(jnp.int32, (SLOTS, SLOTS), 0)
@@ -134,14 +136,14 @@
         block(h, slot, ag_b.at[h, n], ag_r.at[h, slot], sibling).start()
 
     def gather_near(h):
-        @pl.when(between(h, 0, KVH))
+        @pl.when(between(h, 0, EARLY))
         def _():
             for n, i in enumerate((2, -2, 1, -1)):
                 block(h, mine, ag_s.at[h, n], ag_r.at[h, mine], zdev(z + i)).start()
             forward(h, mine, 0)
 
     def gather_far(h):
-        @pl.when(between(h, 0, KVH))
+        @pl.when(between(h, 0, EARLY))
         def _():
             for n, step in enumerate((1, -1)):
                 slot = c * NZ + zmod(z - 2 * step)
@@ -156,7 +158,7 @@
                 forward(h, slot, 3 + n)
 
     def gather_end(h, low):
-        @pl.when(between(h, low, KVH))
+        @pl.when(between(h, low, EARLY))
         def _():
             for n, step in enumerate((1, -1)):
                 slot = c * NZ + zmod(z - 3 * step)
@@ -165,6 +167,30 @@
             slot = c * NZ + zmod(z + 4)
             half_block(h, slot, 0, ag_s.at[h, 6], ag_r.at[h, slot], sibling).wait_recv()
             half_block(h, slot, 1, ag_s.at[h, 7], ag_v.at[h], sibling).wait_recv()
+            forward(h, slot, 7)
+
+    def gather_hop(h, k):
+        @pl.when(between(h, EARLY, KVH))
+        def _():
+            for d in (0, 1):
+                step = 1 - 2 * d
+                slot = c * NZ + zmod(z - step * k)
+                if k:
+                    arrived(h, slot)
+                if k < 3:
+                    block(h, slot, ag_s.at[h, 3 * d + k], ag_r.at[h, slot], zdev(z + step)).start()
+                if k or not d:
+                    forward(h, slot, 3 * d + k)
+            if k == 3:
+                step = 1 - 2 * lax.rem(h, 2)
+                slot = c * NZ + zmod(z - step * 3)
+                block(h, slot, ag_s.at[h, 6], ag_r.at[h, slot], zdev(z + step)).start()
+
+    def gather_last(h):
+        @pl.when(between(h, EARLY, KVH))
+        def _():
+            slot = c * NZ + zmod(z + 4)
+            arrived(h, slot)
             forward(h, slot, 7)
 
     def prepare(h):
@@ -245,9 +271,8 @@
             key = kvb[h, b, 0].astype(f32)
             gk_terms += fold(dk[rows] * key, jnp.sum)
             gq_terms += fold(exact[rows] * key, jnp.sum)
-        remote(
-            acc.at[h, pl.ds(theirs, NZ)], sib.at[h], sl_s.at[h], sl_r.at[h], sibling
-        ).start()
+        slab[h] = acc[h, pl.ds(theirs, NZ)].astype(bf16)
+        remote(slab.at[h], sib.at[h], sl_s.at[h], sl_r.at[h], sibling).start()
         dx, own_terms = norm_grad(kc[:, cols(h)].astype(f32), kg[...], dk[PL:])
         dkc[:, cols(h)] = dx.astype(bf16)
         dvc[:, cols(h)] = dv[PL:].astype(bf16)
@@ -258,60 +283,67 @@
         kt = jnp.concatenate([keys(h, t).T for t in range(NT_)], axis=1)
         dqt = dot(kt, ds[h], NN)
         for g in range(GRP):
-            dy = dqt[:, g * SLOTS : (g + 1) * SLOTS].T * SCALE
             at = cols(h, g, GRP)
-            dx, _ = norm_grad(qv[:, at].astype(f32), qg[...], dy)
-            qv[:, at] = dx.astype(bf16)
+            x = qv[:, at].T.astype(f32)
+            r = lax.rsqrt(jnp.mean(x * x, axis=0, keepdims=True) + EPS)
+            xr = x * r
+            u = dqt[:, g * SLOTS : (g + 1) * SLOTS] * qgt[...]
+            dx = r * (u - xr * jnp.mean(xr * u, axis=0, keepdims=True))
+            qv[:, at] = dx.astype(bf16).T
         dq_copy(h).start()
 
     def dq_copy(h):
         span = pl.ds(pl.multiple_of(h * ROWS, ROWS), ROWS)
         return pltpu.make_async_copy(qv.at[:, span], dq_hbm.at[:, span], dq_sem.at[h])
 
-    def hop(h, d, j):
-        return remote(
-            rss.at[h, d, j], rsr.at[h, d, j], rs_s.at[h, d, j], rs_r.at[h, d, j], zdev(z + 1 - 2 * d)
-        )
+    def part(h, d, k):
+        at = (h, d, k, d) if k == 3 else (h, d, k)
+        reach = (1 - 2 * d) * (1 if k < 2 else 2)
+        return remote(rss.at[at], rsr.at[at], rs_s.at[h, d, k], rs_r.at[h, d, k], zdev(z + reach))
 
     def chip_sum(h, t):
-        return acc[h, c * NZ + t] + sib[h, t]
-
-    def reduce_hop(h, j):
+        return acc[h, c * NZ + t] + sib[h, t].astype(f32)
+
+    def reduce_start(h):
         @pl.when(between(h, 0, KVH))
         def _():
-            odd = lax.rem(h, 2)
-            if j == 4:
-                hop(h, odd, 2).wait_recv()
-                val = chip_sum(h, zmod(z + 1 - 2 * odd)) + rsr[h, odd, 2].astype(f32)
-                rss[h, odd, 3] = val.astype(bf16)
-                hop(h, odd, 3).start()
-                return
-            if j == 1:
-                remote(sib.at[h], sib.at[h], sl_s.at[h], sl_r.at[h], sibling).wait_recv()
-            for d in (0, 1):
-                length = 3 + (odd if d else 1 - odd)
-                val = chip_sum(h, zmod(z + (1 - 2 * d) * (length - j + 1)))
-                if j > 1:
-                    hop(h, d, j - 2).wait_recv()
-                    val = val + rsr[h, d, j - 2].astype(f32)
-                rss[h, d, j - 1] = val.astype(bf16)
-                hop(h, d, j - 1).start()
+            remote(sib.at[h], sib.at[h], sl_s.at[h], sl_r.at[h], sibling).wait_recv()
+            for d, step in ((0, 1), (1, -1)):
+                rss[h, d, 3, d] = chip_sum(h, zmod(z + 4))[d].astype(bf16)
+                part(h, d, 3).start()
+                rss[h, d, 0] = chip_sum(h, zmod(z + 3 * step)).astype(bf16)
+                part(h, d, 0).start()
+            for d, step in ((0, 1), (1, -1)):
+                rss[h, d, 1] = chip_sum(h, zmod(z + step)).astype(bf16)
+                part(h, d, 1).start()
+
+    def reduce_mid(h):
+        @pl.when(between(h, 0, KVH))
+        def _():
+            for d, step in ((0, 1), (1, -1)):
+                part(h, d, 0).wait_recv()
+                part(h, d, 3).wait_recv()
+                val = chip_sum(h, zmod(z + 2 * step)) + rsr[h, d, 0].astype(f32)
+                rss[h, d, 2, 1 - d] = val[1 - d].astype(bf16)
+                rss[h, d, 2, d] = (val[d] + rsr[h, d, 3, d].astype(f32)).astype(bf16)
+                part(h, d, 2).start()
 
     def reduce_end(h):
         @pl.when(between(h, 0, KVH))
         def _():
-            d = lax.rem(h, 2)
-            hop(h, d, 3).wait_recv()
-            hop(h, 1 - d, 2).wait_recv()
-            val = chip_sum(h, z) + (rsr[h, d, 3].astype(f32) + rsr[h, 1 - d, 2].astype(f32))
+            val = chip_sum(h, z)
+            for k in (1, 2):
+                for d in (0, 1):
+                    part(h, d, k).wait_recv()
+                    val = val + rsr[h, d, k].astype(f32)
             dx, _ = norm_grad(kp[:, cols(h)].astype(f32), kg[...], val[0])
             dkp[:, cols(h)] = dx.astype(bf16)
             dvp[:, cols(h)] = val[1].astype(bf16)
 
     def reduce(i):
-        for j in (4, 3, 2, 1):
-            reduce_hop(i - j, j)
-        reduce_end(i - 5)
+        reduce_end(i - 3)
+        reduce_mid(i - 2)
+        reduce_start(i - 1)
 
     base = (0, 2, 10, 14)
 
@@ -349,17 +381,25 @@
         def _():
             gather_far(n - 2)
 
+        @pl.when(n == 2)
+        def _():
+            gather_hop(3, 0)
+
         return carry
 
     lax.fori_loop(0, 4, fill, 0)
     gather_near(2)
     pltpu.make_async_copy(do_hbm, dov, do_sem).wait()
     gather_end(0, 0)
+    gather_hop(3, 1)
+    gather_hop(4, 0)
 
     def main(i, carry):
         gather_end(i + 1, 2)
+        gather_last(i + 1)
         gather_far(i + 2)
-        gather_near(i + 3)
+        for k in (3, 2, 1, 0):
+            gather_hop(i + 5 - k, k)
 
         def between_halves():
             @pl.when(i == 0)
@@ -390,34 +430,32 @@
             def _(i=i):
                 gain_step(i)
 
-        @pl.when(n < 4)
-        def _():
-            queries(2 * n)
-
+        queries(2 * n)
         reduce(KVH + n)
-
-        @pl.when(n < 4)
-        def _():
-            queries(2 * n + 1)
-
+        queries(2 * n + 1)
         return carry
 
-    lax.fori_loop(0, 5, late, 0)
+    lax.fori_loop(0, 4, late, 0)
     total = sum_gains(3)
     gq_out[...] = total[0:1]
     gk_out[...] = total[1:2]
 
     def drain(h, carry):
-        odd = lax.rem(h, 2)
         for d in (0, 1):
-            for k in range(3):
-                hop(h, d, k).wait_send()
-        hop(h, odd, 3).wait_send()
-
+            for k in range(4):
+                part(h, d, k).wait_send()
         for k in range(6):
             block(h, mine, ag_s.at[h, k], ag_r.at[h, mine], sibling).wait_send()
-        for k in (0, 1):
-            half_block(h, mine, k, ag_s.at[h, 6 + k], ag_v.at[h], sibling).wait_send()
+
+        @pl.when(h < EARLY)
+        def _():
+            for k in (0, 1):
+                half_block(h, mine, k, ag_s.at[h, 6 + k], ag_v.at[h], sibling).wait_send()
+
+        @pl.when(h >= EARLY)
+        def _():
+            block(h, mine, ag_s.at[h, 6], ag_r.at[h, mine], sibling).wait_send()
+
         for k in range(NZ):
             block(h, mine, ag_b.at[h, k], ag_r.at[h, mine], sibling).wait_send()
         remote(sib.at[h], sib.at[h], sl_s.at[h], sl_r.at[h], sibling).wait_send()
@@ -454,6 +492,7 @@
             pltpu.VMEM((SLOTS, GRP * wide), bf16),
             pltpu.VMEM((KVH, ROWS, 2 * HD), bf16),
             pltpu.VMEM((KVH, SLOTS, HD), bf16),
+            pltpu.VMEM((HD, SLOTS), f32),
             pltpu.VMEM((SLOTS, CH), f32),
             pltpu.VMEM((KVH, NB, 2, PAGE, HD), bf16),
             pltpu.VMEM((2, KEYS, CH), f32),
@@ -463,7 +502,8 @@
             pltpu.VMEM((KEYS, HD), f32),
             pltpu.VMEM((KEYS, 2 * HD), f32),
             pltpu.VMEM((KVH, NB, 2, PAGE, HD), f32),
-            pltpu.VMEM((KVH, NZ, 2, PAGE, HD), f32),
+            pltpu.VMEM((KVH, NZ, 2, PAGE, HD), bf16),
+            pltpu.VMEM((KVH, NZ, 2, PAGE, HD), bf16),
             pltpu.VMEM((KVH, 2, 4, 2, PAGE, HD), bf16),
             pltpu.VMEM((KVH, 2, 4, 2, PAGE, HD), bf16),
             pltpu.VMEM((8, HD), f32),

time: 94.1 us -> 93.9 us (level); the launches traced: 94 us -> 92.2 us
  Pallas kernels: 93.3 us -> 91.6 us
    pallas_call x1, Pallas kernels: 89.4 us -> 87.7 us  [body(): pl.pallas_call(kernel, out_shape=(shape((SLOTS, GRP * wide), bf16), shape...]
where the time goes in v3:
time: 93.9 us; the launch traced here: 92.2 us
  Pallas kernels  91.6 us (98%)
    pallas_call x1, Pallas kernels, body(): pl.pallas_call(kernel, out_shape=(shape((SLOTS, GRP * wide), bf16), shape...  87.7 us
    pallas_call x1, Pallas kernels, finish(): pl.pallas_call(finish_kernel, out_shape=[jax.ShapeDtypeStruct(x.shape, x....  3.92 us

profile of v3, /device:TPU:1, one launch (start us, length us, event | category | flops | bytes accessed | tf_op | source)
XLA Modules:
  0.0 92.2 jit_solution(5937747636542963685)
XLA Ops:
  0.6 87.7 %attention_backward.1 = (bf16[128,8192]{1,0:T(8,128)(2,1)}, bf16[128,1024]{1,0:T(8,128)(2,1)}, bf16[128,1024]{1,0:T(8,128)(2,1)}, bf16[64,1024]{1,0:T(8,128)(2,1...) custom-call(bf16[128,8192]{1,0:T(8,128)(2,1)} %bitcast.16, bf16[128,8192]{1,0:T(8,128)(2,1)} %bitcast.17, ...), custom_call_target="tpu_custom_call" | custom-call | flops 12999999488 | bytes 8388608 | tf_op jit(solution)/shard_map/attention_backward/pallas_call | solution.py:477
  88.3 3.9 %finish.1 = (bf16[128,8192]{1,0:T(8,128)(2,1)}, bf16[128,1024]{1,0:T(8,128)(2,1)}, bf16[128,1024]{1,0:T(8,128)(2,1)}, bf16[64,1024]{1,0:T(8,128)(2,1)}, bf16[64,...) custom-call(bf16[128,8192]{1,0:T(8,128)(2,1)} %get-tuple-element.21.refs_0_, ...), custom_call_target="tpu_custom_call" | custom-call | tf_op jit(solution)/shard_map/finish/pallas_call | solution.py:560
